TPU v7x, 32 devices: a whole 2x2x4 slice. The times are simulated.
32 devices in a mesh: groups: 2 (over y), epoch: 4 (over x, core), tile: 4 (over z).
Axes of the slice: x: 2, y: 2, z: 4, core: 2. Of those that a mesh axis runs over, the one named last changes fastest.
Arguments:
- east_velocity: float32 [256, 16, 2048], P('epoch', ('groups', 'tile')), parts along dimension 1, may hold values from -6 to 6
- up_velocity: float32 [256, 16, 2048], P('epoch', ('groups', 'tile')), parts along dimension 1, may hold values from -6 to 6
- metric_table: float32 [64], replicated, may hold values from 1 to 3
- lat_index: int32 [16], P(('groups', 'tile')), parts along dimension 0, may hold values from 0 to 63
- coherent: int32 [16, 2048], P(('groups', 'tile'), 'epoch'), parts along dimension 0, may hold values 0 or 1
Outputs:
- rfactor: float32 [512, 256], P('groups'), parts along dimension 0
- scores: float32 [3, 256, 16, 2048], P(None, None, ('groups', 'tile'), 'epoch'), parts along dimension 2
There are 2 independent parts, one for each index of `groups`. A program takes and returns all parts, laid end to end along the dimension named above; an argument that names none is the same for every part. Nothing has to cross between parts.
All inputs are finite; a program needn't handle non-finite values. No bound on the sum of `coherent` on one device may be relied on, other than what follows from the above.
Results may differ from a plain program's by a relative error of at most 0.00013.
Values sent between devices are 32-bit elements; how exact they have to be, the bound alone decides.
A program may use at most 64 MiB of HBM per device.

v0:
```python
import functools

import jax
import jax.numpy as jnp
from jax import lax
from jax.experimental import pallas as pl
from jax.experimental.pallas import tpu as pltpu
from jax.sharding import PartitionSpec as P

MESH = pl.DeviceIdType.MESH
HIGHEST = lax.Precision.HIGHEST
LANES = 128
LEAF = 32
SUB = 8
VMEM_LIMIT = 48 * 1024 * 1024


def exchange_kernel(
    count_e, count_z, v_ref, edge_ref, buf_ref, col_ref,
    send, recv, edge_send, edge_recv, z_send, z_recv, local,
):
    g, e, z = lax.axis_index("groups"), lax.axis_index("epoch"), lax.axis_index("tile")
    fields, rows, te, columns = v_ref.shape
    wc = columns // count_e
    has_down, has_up = z > 0, z < count_z - 1

    barrier = pltpu.get_barrier_semaphore()
    for d in range(1, count_e):
        pl.semaphore_signal(barrier, inc=1, device_id=(g, (e + d) % count_e, z), device_id_type=MESH)

    @pl.when(has_down)
    def _():
        pl.semaphore_signal(barrier, inc=1, device_id=(g, e, z - 1), device_id_type=MESH)

    @pl.when(has_up)
    def _():
        pl.semaphore_signal(barrier, inc=1, device_id=(g, e, z + 1), device_id_type=MESH)

    neighbours = lax.div(z + count_z - 1, count_z) + lax.div(2 * (count_z - 1) - z, count_z)
    pl.semaphore_wait(barrier, count_e - 1 + neighbours)

    def cols(who):
        return pl.ds(pl.multiple_of(who * wc, LANES), wc)

    def times(who):
        return pl.ds(pl.multiple_of(who * te, 8), te)

    chunks = [(r, f) for r in range(rows) for f in range(fields)]

    def across(d, c):
        r, f = chunks[c]
        to = (e + d) % count_e
        return pltpu.make_async_remote_copy(
            src_ref=v_ref.at[f, r, :, cols(to)],
            dst_ref=buf_ref.at[f, r + 1, times(e), :],
            send_sem=send.at[d, c], recv_sem=recv.at[d, c],
            device_id=(g, to, z), device_id_type=MESH,
        )

    def edges(d):
        to = (e + d) % count_e
        return pltpu.make_async_remote_copy(
            src_ref=edge_ref.at[to], dst_ref=col_ref.at[times(e), :],
            send_sem=edge_send.at[d], recv_sem=edge_recv.at[d],
            device_id=(g, to, z), device_id_type=MESH,
        )

    def beside(d, f, up):
        source = (e + count_e - d) % count_e
        r = rows - 1 if up else 0
        src = v_ref.at[f, r, :, cols(e)] if d == 0 else buf_ref.at[f, r + 1, times(source), :]
        side = 1 if up else 0
        return pltpu.make_async_remote_copy(
            src_ref=src, dst_ref=buf_ref.at[f, 0 if up else rows + 1, times(source), :],
            send_sem=z_send.at[side, d, f], recv_sem=z_recv.at[side, d, f],
            device_id=(g, e, z + 1 if up else z - 1), device_id_type=MESH,
        )

    def forward(d, c):
        r, f = chunks[c]
        if r == 0:
            @pl.when(has_down)
            def _():
                beside(d, f, False).start()
        if r == rows - 1:
            @pl.when(has_up)
            def _():
                beside(d, f, True).start()

    own = []
    for c in range(len(chunks)):
        for d in range(1, count_e):
            across(d, c).start()
        forward(0, c)
        r, f = chunks[c]
        own.append(pltpu.make_async_copy(
            v_ref.at[f, r, :, cols(e)], buf_ref.at[f, r + 1, times(e), :], local.at[c]))
        own[-1].start()
    for d in range(1, count_e):
        edges(d).start()
    own.append(pltpu.make_async_copy(edge_ref.at[e], col_ref.at[times(e), :], local.at[len(chunks)]))
    own[-1].start()

    for c in range(len(chunks)):
        for d in range(1, count_e):
            across(d, c).wait_recv()
            forward(d, c)
    for d in range(1, count_e):
        edges(d).wait()
        for c in range(len(chunks)):
            across(d, c).wait_send()
    for copy in own:
        copy.wait()

    @pl.when(has_down)
    def _():
        for d in range(count_e):
            for f in range(fields):
                beside(d, f, False).wait_send()
                beside(d, f, True).wait_recv()

    @pl.when(has_up)
    def _():
        for d in range(count_e):
            for f in range(fields):
                beside(d, f, True).wait_send()
                beside(d, f, False).wait_recv()


def exchange(velocity, edge, count_e, count_z):
    fields, rows, te, columns = velocity.shape
    wc = columns // count_e
    n = fields * rows
    dma = pltpu.SemaphoreType.DMA
    return pl.pallas_call(
        functools.partial(exchange_kernel, count_e, count_z),
        out_shape=(
            jax.ShapeDtypeStruct((fields, rows + 2, te * count_e, wc), jnp.float32),
            jax.ShapeDtypeStruct((te * count_e, LANES), jnp.float32),
        ),
        in_specs=[pl.BlockSpec(memory_space=pl.ANY)] * 2,
        out_specs=(pl.BlockSpec(memory_space=pl.ANY),) * 2,
        scratch_shapes=[
            dma((count_e, n)), dma((count_e, n)), dma((count_e,)), dma((count_e,)),
            dma((2, count_e, fields)), dma((2, count_e, fields)), dma((n + 1,)),
        ],
        compiler_params=pltpu.CompilerParams(collective_id=0, has_side_effects=True),
        name="exchange",
    )(velocity, edge)


def nt(a, b):
    return lax.dot_general(
        a, b, (((1,), (1,)), ((), ())), precision=HIGHEST, preferred_element_type=jnp.float32)


def series_kernel(count_z, lat_ref, table_ref, coh_ref, buf_ref, col_ref, s_ref, gram_ref):
    z = lax.axis_index("tile")
    _, padded_rows, epochs, wc = buf_ref.shape
    rows = padded_rows - 2
    lane = lax.broadcasted_iota(jnp.int32, (epochs, wc), 1)
    steps = lax.broadcasted_iota(jnp.int32, (epochs, 1), 0).astype(jnp.float32) - (epochs - 1) / 2.0
    squares = epochs * (epochs * epochs - 1) / 12.0

    def along_x(f, r):
        x = buf_ref[f, r + 1]
        at = (f * rows + r) * 2
        right = jnp.where(lane == wc - 1, col_ref[:, at + 1:at + 2], pltpu.roll(x, wc - 1, 1))
        left = jnp.where(lane == 0, col_ref[:, at:at + 1], pltpu.roll(x, 1, 1))
        return 0.5 * (right - left)

    def row(f, i):
        x = buf_ref[f, i]
        if i == 0:
            x = jnp.where(z > 0, x, 0.0)
        if i == rows + 1:
            x = jnp.where(z < count_z - 1, x, 0.0)
        return x

    def along_y(f, r):
        return 0.5 * (row(f, r + 2) - row(f, r))

    total = None
    for r in range(rows):
        m = table_ref[lat_ref[r]]
        mask = coh_ref[r:r + 1, :].astype(jnp.float32)
        for k in range(3):
            if k == 0:
                strain = m * along_x(0, r)
            elif k == 1:
                strain = along_y(0, r)
            else:
                strain = m * along_x(1, r) + along_y(1, r)
            center = jnp.sum(strain, axis=0, keepdims=True) * (1.0 / epochs)
            slope = jnp.sum(strain * steps, axis=0, keepdims=True) * (1.0 / squares)
            series = (strain - center - slope * steps) * mask
            s_ref[k, r] = series
            part = nt(series, series)
            total = part if total is None else total + part
    gram_ref[...] = total


def make_series(lat_index, metric_table, coherent, buf, col, count_z):
    fields, padded_rows, epochs, wc = buf.shape
    smem, vmem = pl.BlockSpec(memory_space=pltpu.SMEM), pl.BlockSpec(memory_space=pltpu.VMEM)
    return pl.pallas_call(
        functools.partial(series_kernel, count_z),
        out_shape=(
            jax.ShapeDtypeStruct((3, padded_rows - 2, epochs, wc), jnp.float32),
            jax.ShapeDtypeStruct((epochs, epochs), jnp.float32),
        ),
        in_specs=[smem, smem, vmem, vmem, vmem],
        out_specs=(vmem, vmem),
        compiler_params=pltpu.CompilerParams(vmem_limit_bytes=VMEM_LIMIT),
        name="series",
    )(lat_index, metric_table, coherent, buf, col)


def reduce_kernel(count_e, count_z, x_ref, o_ref, parts, sums, full, s1, r1, s2, r2, s3, r3):
    g, e, z = lax.axis_index("groups"), lax.axis_index("epoch"), lax.axis_index("tile")
    size = x_ref.shape[0] // count_e

    def rows(who):
        return pl.ds(pl.multiple_of(who * size, 8), size)

    barrier = pltpu.get_barrier_semaphore()
    for d in range(1, count_e):
        pl.semaphore_signal(barrier, inc=1, device_id=(g, (e + d) % count_e, z), device_id_type=MESH)
    for d in range(1, count_z):
        pl.semaphore_signal(barrier, inc=1, device_id=(g, e, (z + d) % count_z), device_id_type=MESH)
    pl.semaphore_wait(barrier, count_e + count_z - 2)

    def scatter(d):
        to = (e + d) % count_e
        return pltpu.make_async_remote_copy(
            src_ref=x_ref.at[rows(to), :], dst_ref=parts.at[d], send_sem=s1.at[d], recv_sem=r1.at[d],
            device_id=(g, to, z), device_id_type=MESH)

    def share(d):
        to = (z + d) % count_z
        return pltpu.make_async_remote_copy(
            src_ref=sums.at[0], dst_ref=sums.at[d], send_sem=s2.at[d], recv_sem=r2.at[d],
            device_id=(g, e, to), device_id_type=MESH)

    def gather(d):
        to = (e + d) % count_e
        return pltpu.make_async_remote_copy(
            src_ref=full.at[rows(e), :], dst_ref=full.at[rows(e), :], send_sem=s3.at[d], recv_sem=r3.at[d],
            device_id=(g, to, z), device_id_type=MESH)

    for d in range(1, count_e):
        scatter(d).start()
    total = x_ref[rows(e), :]
    for d in range(1, count_e):
        scatter(d).wait_recv()
        total = total + parts[d]
    sums[0] = total
    for d in range(1, count_z):
        share(d).start()
    for d in range(1, count_z):
        share(d).wait_recv()
    total = None
    for i in range(count_z):
        part = sums[(z + count_z - i) % count_z]
        total = part if total is None else total + part
    full[rows(e), :] = total
    for d in range(1, count_e):
        gather(d).start()
    for d in range(1, count_e):
        gather(d).wait_recv()
    o_ref[...] = full[...]
    for d in range(1, count_e):
        scatter(d).wait_send()
        gather(d).wait_send()
    for d in range(1, count_z):
        share(d).wait_send()


def reduce_gram(gram, count_e, count_z):
    n = gram.shape[0]
    size = n // count_e
    dma = pltpu.SemaphoreType.DMA
    vmem = pl.BlockSpec(memory_space=pltpu.VMEM)
    return pl.pallas_call(
        functools.partial(reduce_kernel, count_e, count_z),
        out_shape=jax.ShapeDtypeStruct((n, n), jnp.float32),
        in_specs=[vmem],
        out_specs=vmem,
        scratch_shapes=[
            pltpu.VMEM((count_e, size, n), jnp.float32),
            pltpu.VMEM((count_z, size, n), jnp.float32),
            pltpu.VMEM((n, n), jnp.float32),
            dma((count_e,)), dma((count_e,)), dma((count_z,)), dma((count_z,)),
            dma((count_e,)), dma((count_e,)),
        ],
        compiler_params=pltpu.CompilerParams(collective_id=1, has_side_effects=True),
        name="reduce_gram",
    )(gram)


def leaf_inverse(block):
    n = block.shape[0]
    i = lax.broadcasted_iota(jnp.int32, (n, LANES), 0)
    j = lax.broadcasted_iota(jnp.int32, (n, LANES), 1)
    eye = (j == i + n).astype(jnp.float32)
    pad = jnp.zeros((n, LANES - n), jnp.float32)
    work = jnp.concatenate([block, pad], axis=1) + eye
    pivots = jnp.ones((n, LANES), jnp.float32)
    for start in range(0, n, SUB):
        held = [jnp.broadcast_to(work[:, c:c + 1], (n, LANES)) for c in range(start, start + SUB)]
        for c in range(start, start + SUB):
            column = held[c - start]
            pivot = column[c:c + 1, :]
            factor = jnp.where(i > c, column * (1.0 / pivot), 0.0)
            pivots = jnp.where(i == c, pivot, pivots)
            for k in range(c + 1, start + SUB):
                held[k - start] = held[k - start] - factor * held[k - start][c:c + 1, :]
            work = work - factor * work[c:c + 1, :]
    return (work * lax.rsqrt(pivots))[:, n:2 * n]


def scores_kernel(count, s_ref, gram_ref, r_ref, out_ref, work):
    epochs = gram_ref.shape[0]
    rows, wc = s_ref.shape[1], s_ref.shape[3]
    i = lax.broadcasted_iota(jnp.int32, (epochs, epochs), 0)
    j = lax.broadcasted_iota(jnp.int32, (epochs, epochs), 1)
    eye = (i == j).astype(jnp.float32)
    work[:, :epochs] = gram_ref[...] * (1.0 / count) + 0.05 * eye
    work[:, epochs:] = eye
    for start in range(0, epochs, LEAF):
        stop = start + LEAF
        inner = leaf_inverse(work[start:stop, start:stop])
        rows_now = jnp.dot(inner, work[start:stop, :], precision=HIGHEST, preferred_element_type=jnp.float32)
        work[start:stop, :] = rows_now
        if stop < epochs:
            head = rows_now[:, :epochs]
            update = lax.dot_general(
                head, rows_now, (((0,), (0,)), ((), ())), precision=HIGHEST,
                preferred_element_type=jnp.float32)
            work[stop:, :] = work[stop:, :] - update[stop:, :]
    r_ref[...] = jnp.where(i <= j, work[:, :epochs], 0.0)
    whiten = jnp.where(i >= j, work[:, epochs:], 0.0)
    tiles = wc // LANES
    for k in range(3):
        for r in range(rows):
            result = jnp.dot(whiten, s_ref[k, r], precision=HIGHEST, preferred_element_type=jnp.float32)
            for c in range(tiles):
                out_ref[k, pl.ds(c * rows + r, epochs, stride=tiles * rows), :] = result[:, c * LANES:(c + 1) * LANES]


def make_scores(series, gram, count):
    _, rows, epochs, wc = series.shape
    vmem = pl.BlockSpec(memory_space=pltpu.VMEM)
    rfactor, scores = pl.pallas_call(
        functools.partial(scores_kernel, count),
        out_shape=(
            jax.ShapeDtypeStruct((epochs, epochs), jnp.float32),
            jax.ShapeDtypeStruct((3, epochs * rows * wc // LANES, LANES), jnp.float32),
        ),
        in_specs=[vmem, vmem],
        out_specs=(vmem, vmem),
        scratch_shapes=[pltpu.VMEM((epochs, 2 * epochs), jnp.float32)],
        compiler_params=pltpu.CompilerParams(vmem_limit_bytes=VMEM_LIMIT),
        name="scores",
    )(series, gram)
    scores = scores.reshape(3, epochs, wc // LANES, rows, LANES)
    return rfactor, scores.transpose(0, 1, 3, 2, 4).reshape(3, epochs, rows, wc)


def on_device(count_e, count_z, east_velocity, up_velocity, metric_table, lat_index, coherent):
    velocity = jnp.stack([east_velocity, up_velocity]).transpose(0, 2, 1, 3)
    fields, rows, te, columns = velocity.shape
    wc = columns // count_e
    blank = jnp.zeros((fields, rows, te, 1), jnp.float32)
    left = jnp.concatenate([blank, velocity[..., wc - 1:columns - 1:wc]], axis=3)
    right = jnp.concatenate([velocity[..., wc:columns:wc], blank], axis=3)
    edge = jnp.stack([left, right], axis=2).reshape(2 * fields * rows, te, count_e).transpose(2, 1, 0)
    edge = jnp.pad(edge, ((0, 0), (0, 0), (0, LANES - 2 * fields * rows)))
    buf, col = exchange(velocity, edge, count_e, count_z)
    series, gram = make_series(lat_index, metric_table, coherent, buf, col, count_z)
    gram = reduce_gram(gram, count_e, count_z)
    return make_scores(series, gram, 3 * rows * count_z * columns)


def solution(mesh):
    in_specs = (
        P("epoch", ("groups", "tile"), None),
        P("epoch", ("groups", "tile"), None),
        P(),
        P(("groups", "tile")),
        P(("groups", "tile"), "epoch"),
    )
    out_specs = (P("groups", None), P(None, None, ("groups", "tile"), "epoch"))
    return jax.shard_map(
        functools.partial(on_device, mesh.shape["epoch"], mesh.shape["tile"]),
        mesh=mesh, in_specs=in_specs, out_specs=out_specs, check_vma=False,
    )
```

profile of v0, /device:TPU:0, one launch (start us, length us, event | category | flops | bytes accessed | tf_op | source)
XLA Modules:
  0.0 88.3 jit_solution(1880477016785936220)
XLA Ops:
  0.6 2.8 %copy_bitcast_fusion = (f32[1,64,2,2048]{3,1,2,0:T(8,128)S(1)}, f32[1,64,2,2048]{3,1,2,0:T(8,128)S(1)}) fusion(f32[64,2,2048]{2,1,0:T(2,128)} %param.6, f32[64,2,2048]{2,1,0:T(2,128)} %param.5), kind=kLoop, calls=%fused_computation.1 | loop fusion | bytes 4194304 | tf_op jit(solution)/shard_map/stack | solution.py:371
  3.4 0.1 maximum_bitcast_fusion.v_ref
  3.5 0.0 copy-start.6
  3.5 0.4 slice.7
  3.9 0.0 copy-start.3
  3.9 0.0 copy-start.4
  4.0 0.0 copy-start.5
  4.0 0.4 slice.6
  4.4 0.1 pad_bitcast_fusion.1
  4.5 0.1 copy.25
  4.7 0.1 copy.26
  4.8 0.7 pad.6.edge_ref
  5.4 0.0 copy-done.6
  5.5 36.5 %exchange.1 = (f32[2,4,256,512]{3,2,1,0:T(8,128)}, f32[256,128]{1,0:T(8,128)}) custom-call(f32[2,2,64,2048]{3,2,1,0:T(8,128)} %copy-done.6, f32[4,64,128]{2,1,0:T(8,128)} %pad.6.edge_ref), custom_call_target="tpu_custom_call" | custom-call | tf_op jit(solution)/shard_map/exchange/pallas_call | solution.py:135
  41.9 0.0 copy-done.3
  42.0 0.0 copy-done.4
  42.0 0.9 %copy-done.2 = f32[256,128]{1,0:T(8,128)S(1)} copy-done((f32[256,128]{1,0:T(8,128)S(1)}, f32[256,128]{1,0:T(8,128)}, u32[]{:S(2)}) %copy-start.2) | copy-done | bytes 131096
  42.9 6.5 %series.1 = (f32[3,2,256,512]{3,2,1,0:T(8,128)S(1)}, f32[256,256]{1,0:T(8,128)S(1)}) custom-call(s32[2]{0:T(128)S(1)} %copy-done.4, f32[64]{0:T(128)S(1)} %copy-done.5, s32[2,512]{1,0:T(2,128)S(1)} %copy-done.3, f32[2,4,256,512]{3,2,1,0:T(8,128)} %get-tuple-element.8.buf_ref, f32[256,128]{1,0:T(8,128)S(1)} %copy-done.2), custom_call_target="tpu_custom_call" | custom-call | tf_op jit(solution)/shard_map/series/pallas_call | solution.py:206
  49.4 0.0 copy-start.1
  49.4 0.7 copy-done.1
  50.1 20.2 %reduce_gram.1.gram_ref = f32[256,256]{1,0:T(8,128)} custom-call(f32[256,256]{1,0:T(8,128)} %copy-done.1), custom_call_target="tpu_custom_call" | custom-call | tf_op jit(solution)/shard_map/reduce_gram/pallas_call | solution.py:284
  70.3 0.0 copy-start
  70.4 0.9 %copy-done = f32[256,256]{1,0:T(8,128)S(1)} copy-done((f32[256,256]{1,0:T(8,128)S(1)}, f32[256,256]{1,0:T(8,128)}, u32[]{:S(2)}) %copy-start) | copy-done | bytes 262168
  71.3 17.0 %scores.1 = (f32[256,256]{1,0:T(8,128)}, f32[3,2048,128]{2,1,0:T(8,128)}) custom-call(f32[3,2,256,512]{3,2,1,0:T(8,128)S(1)} %get-tuple-element.10.s_ref, f32[256,256]{1,0:T(8,128)S(1)} %copy-done), custom_call_target="tpu_custom_call" | custom-call | tf_op jit(solution)/shard_map/scores/pallas_call | solution.py:354
  (4 shorter events, 0.0 us)
Async XLA Ops:
  3.5 1.9 %copy-start.6 = (f32[2,2,64,2048]{3,2,1,0:T(8,128)}, f32[2,2,64,2048]{3,2,1,0:T(8,128)S(1)}, u32[]{:S(2)}) copy-start(f32[2,2,64,2048]{3,2,1,0:T(8,128)S(1)} %maximum_bitcast_fusion.v_ref) | copy-start | bytes 6291460
  3.9 38.0 %copy-start.3 = (s32[2,512]{1,0:T(2,128)S(1)}, s32[2,512]{1,0:T(2,128)}, u32[]{:S(2)}) copy-start(s32[2,512]{1,0:T(2,128)} %coh_ref.1) | copy-start | bytes 12292
  3.9 38.0 %copy-start.4 = (s32[2]{0:T(128)S(1)}, s32[2]{0:T(128)}, u32[]{:S(2)}) copy-start(s32[2]{0:T(128)} %lat_ref.1) | copy-start | bytes 28
  4.0 38.0 %copy-start.5 = (f32[64]{0:T(128)S(1)}, f32[64]{0:T(128)}, u32[]{:S(2)}) copy-start(f32[64]{0:T(128)} %table_ref.1) | copy-start | bytes 772
  42.0 0.9 %copy-start.2 = (f32[256,128]{1,0:T(8,128)S(1)}, f32[256,128]{1,0:T(8,128)}, u32[]{:S(2)}) copy-start(f32[256,128]{1,0:T(8,128)} %get-tuple-element.9.col_ref) | copy-start | bytes 393220
  49.4 0.7 copy-start.1
  70.3 1.0 %copy-start = (f32[256,256]{1,0:T(8,128)S(1)}, f32[256,256]{1,0:T(8,128)}, u32[]{:S(2)}) copy-start(f32[256,256]{1,0:T(8,128)} %reduce_gram.1.gram_ref) | copy-start | bytes 786436
where the time goes:
time: 88.7 us; the launch traced here: 88.3 us
  Pallas kernels  80.3 us (91%)
  local copies, waits for them, and re-layouts  7.11 us (8%)
    pallas_call x1, Pallas kernels, exchange(): pl.pallas_call(functools.partial(exchange_kernel, count_e, count_z), out_...  36.5 us
    pallas_call x1, Pallas kernels, reduce_gram(): pl.pallas_call(functools.partial(reduce_kernel, count_e, count_z), out_sh...  20.2 us
    pallas_call x1, Pallas kernels, make_scores(): pl.pallas_call(functools.partial(scores_kernel, count), out_shape=(jax.Sh...  17 us
    pallas_call x1, Pallas kernels, make_series(): pl.pallas_call(functools.partial(series_kernel, count_z), out_shape=(jax....  6.51 us
    another operation x1, local copies, waits for them, and re-layouts, on_device(): velocity = jnp.stack([east_velocity, up_velocity]).transpose(0, 2, 1, 3)  2.76 us
    unnamed x14, local copies, waits for them, and re-layouts  2.56 us

commit v1 on v0

v1 whole, which is shorter than its diff:
```python
import functools

import jax
import jax.numpy as jnp
from jax import lax
from jax.experimental import pallas as pl
from jax.experimental.pallas import tpu as pltpu
from jax.sharding import PartitionSpec as P

MESH = pl.DeviceIdType.MESH
HIGHEST = lax.Precision.HIGHEST
LANES = 128
LEAF = 32
SUB = 8
PIECES = 2
WINDOW = 2
VMEM_LIMIT = 48 * 1024 * 1024


def exchange_kernel(
    count_e, count_z, v_ref, edge_ref, buf_ref, col_ref,
    send, recv, edge_send, edge_recv, z_send, z_recv, local,
):
    g, e, z = lax.axis_index("groups"), lax.axis_index("epoch"), lax.axis_index("tile")
    fields, rows, te, columns = v_ref.shape
    wc = columns // count_e
    has_down, has_up = z > 0, z < count_z - 1

    barrier = pltpu.get_barrier_semaphore()
    for d in range(1, count_e):
        pl.semaphore_signal(barrier, inc=1, device_id=(g, (e + d) % count_e, z), device_id_type=MESH)

    @pl.when(has_down)
    def _():
        pl.semaphore_signal(barrier, inc=1, device_id=(g, e, z - 1), device_id_type=MESH)

    @pl.when(has_up)
    def _():
        pl.semaphore_signal(barrier, inc=1, device_id=(g, e, z + 1), device_id_type=MESH)

    neighbours = lax.div(z + count_z - 1, count_z) + lax.div(2 * (count_z - 1) - z, count_z)
    pl.semaphore_wait(barrier, count_e - 1 + neighbours)

    def cols(who):
        return pl.ds(pl.multiple_of(who * wc, LANES), wc)

    def times(who):
        return pl.ds(pl.multiple_of(who * te, 8), te)

    chips = count_e // 2
    chip, core = lax.div(e, 2), lax.rem(e, 2)

    def target(d):
        return lax.rem(chip + d // 2, chips) * 2 + lax.rem(core + d % 2, 2)

    def origin(d):
        return lax.rem(chip + chips - d // 2, chips) * 2 + lax.rem(core + d % 2, 2)

    chunks = [(r, f, h) for h in range(PIECES) for f in range(fields) for r in range(rows)]
    piece = te // PIECES

    def some(who, h):
        return pl.ds(pl.multiple_of(who * te + h * piece, 8), piece)

    def across(d, c):
        r, f, h = chunks[c]
        to = target(d)
        return pltpu.make_async_remote_copy(
            src_ref=v_ref.at[f, r, pl.ds(h * piece, piece), cols(to)],
            dst_ref=buf_ref.at[f, r + 1, some(e, h), :],
            send_sem=send.at[d, c], recv_sem=recv.at[d, c],
            device_id=(g, to, z), device_id_type=MESH,
        )

    def edges(d):
        to = target(d)
        return pltpu.make_async_remote_copy(
            src_ref=edge_ref.at[to], dst_ref=col_ref.at[times(e), :],
            send_sem=edge_send.at[d], recv_sem=edge_recv.at[d],
            device_id=(g, to, z), device_id_type=MESH,
        )

    def beside(d, f, h, up):
        r = rows - 1 if up else 0
        where = some(origin(d), h)
        src = v_ref.at[f, r, pl.ds(h * piece, piece), cols(e)] if d == 0 else buf_ref.at[f, r + 1, where, :]
        side = 1 if up else 0
        return pltpu.make_async_remote_copy(
            src_ref=src, dst_ref=buf_ref.at[f, 0 if up else rows + 1, where, :],
            send_sem=z_send.at[side, d, f * PIECES + h], recv_sem=z_recv.at[side, d, f * PIECES + h],
            device_id=(g, e, z + 1 if up else z - 1), device_id_type=MESH,
        )

    def forward(d, c):
        r, f, h = chunks[c]
        if r == 0:
            @pl.when(has_down)
            def _():
                beside(d, f, h, False).start()
        if r == rows - 1:
            @pl.when(has_up)
            def _():
                beside(d, f, h, True).start()

    far = range(2, count_e)
    for c in range(min(WINDOW, len(chunks))):
        for d in far:
            across(d, c).start()
    for d in range(1, count_e):
        edges(d).start()
    for c in range(len(chunks)):
        across(1, c).start()
    for c in range(len(chunks)):
        forward(0, c)
    own = []
    for f in range(fields):
        for r in range(rows):
            own.append(pltpu.make_async_copy(
                v_ref.at[f, r, :, cols(e)], buf_ref.at[f, r + 1, times(e), :], local.at[f * rows + r]))
    own.append(pltpu.make_async_copy(edge_ref.at[e], col_ref.at[times(e), :], local.at[fields * rows]))
    for copy in own:
        copy.start()
    for c in range(len(chunks)):
        across(1, c).wait_recv()
        forward(1, c)
    for c in range(len(chunks)):
        for d in far:
            across(d, c).wait_recv()
            forward(d, c)
            if c + WINDOW < len(chunks):
                across(d, c + WINDOW).start()
    for d in range(1, count_e):
        edges(d).wait()
        for c in range(len(chunks)):
            across(d, c).wait_send()
    for copy in own:
        copy.wait()

    halves = [(d, f, h) for d in range(count_e) for f in range(fields) for h in range(PIECES)]

    @pl.when(has_down)
    def _():
        for d, f, h in halves:
            beside(d, f, h, False).wait_send()
            beside(d, f, h, True).wait_recv()

    @pl.when(has_up)
    def _():
        for d, f, h in halves:
            beside(d, f, h, True).wait_send()
            beside(d, f, h, False).wait_recv()


def exchange(velocity, edge, count_e, count_z):
    fields, rows, te, columns = velocity.shape
    wc = columns // count_e
    n = fields * rows
    dma = pltpu.SemaphoreType.DMA
    return pl.pallas_call(
        functools.partial(exchange_kernel, count_e, count_z),
        out_shape=(
            jax.ShapeDtypeStruct((fields, rows + 2, te * count_e, wc), jnp.float32),
            jax.ShapeDtypeStruct((te * count_e, LANES), jnp.float32),
        ),
        in_specs=[pl.BlockSpec(memory_space=pl.ANY)] * 2,
        out_specs=(pl.BlockSpec(memory_space=pl.ANY),) * 2,
        scratch_shapes=[
            dma((count_e, n * PIECES)), dma((count_e, n * PIECES)), dma((count_e,)), dma((count_e,)),
            dma((2, count_e, fields * PIECES)), dma((2, count_e, fields * PIECES)), dma((n + 1,)),
        ],
        compiler_params=pltpu.CompilerParams(collective_id=0, has_side_effects=True),
        name="exchange",
    )(velocity, edge)


def nt(a, b):
    return lax.dot_general(
        a, b, (((1,), (1,)), ((), ())), precision=HIGHEST, preferred_element_type=jnp.float32)


def series_kernel(
    count_e, count_z, lat_ref, table_ref, coh_ref, buf_ref, col_ref, s_ref, gram_ref,
    packed, parts, sums, s1, r1, s2, r2, s3, r3,
):
    g, e, z = lax.axis_index("groups"), lax.axis_index("epoch"), lax.axis_index("tile")
    barrier = pltpu.get_barrier_semaphore()
    for d in range(1, count_e):
        pl.semaphore_signal(barrier, inc=1, device_id=(g, (e + d) % count_e, z), device_id_type=MESH)
    for d in range(1, count_z):
        pl.semaphore_signal(barrier, inc=1, device_id=(g, e, (z + d) % count_z), device_id_type=MESH)
    _, padded_rows, epochs, wc = buf_ref.shape
    rows = padded_rows - 2
    lane = lax.broadcasted_iota(jnp.int32, (epochs, wc), 1)
    steps = lax.broadcasted_iota(jnp.int32, (epochs, 1), 0).astype(jnp.float32) - (epochs - 1) / 2.0
    squares = epochs * (epochs * epochs - 1) / 12.0

    def along_x(f, r):
        x = buf_ref[f, r + 1]
        at = (f * rows + r) * 2
        right = jnp.where(lane == wc - 1, col_ref[:, at + 1:at + 2], pltpu.roll(x, wc - 1, 1))
        left = jnp.where(lane == 0, col_ref[:, at:at + 1], pltpu.roll(x, 1, 1))
        return 0.5 * (right - left)

    def row(f, i):
        x = buf_ref[f, i]
        if i == 0:
            x = jnp.where(z > 0, x, 0.0)
        if i == rows + 1:
            x = jnp.where(z < count_z - 1, x, 0.0)
        return x

    def along_y(f, r):
        return 0.5 * (row(f, r + 2) - row(f, r))

    total = None
    for r in range(rows):
        m = table_ref[lat_ref[r]]
        mask = coh_ref[r:r + 1, :].astype(jnp.float32)
        for k in range(3):
            if k == 0:
                strain = m * along_x(0, r)
            elif k == 1:
                strain = along_y(0, r)
            else:
                strain = m * along_x(1, r) + along_y(1, r)
            center = jnp.sum(strain, axis=0, keepdims=True) * (1.0 / epochs)
            slope = jnp.sum(strain * steps, axis=0, keepdims=True) * (1.0 / squares)
            series = (strain - center - slope * steps) * mask
            s_ref[k, r] = series
            part = nt(series, series)
            total = part if total is None else total + part
    for at, (bi, bj) in enumerate(packed_blocks(epochs)):
        packed[at * LANES:(at + 1) * LANES, :] = total[bi * LANES:(bi + 1) * LANES, bj * LANES:(bj + 1) * LANES]

    size = packed.shape[0] // count_e

    def rows_of(who):
        return pl.ds(pl.multiple_of(who * size, 8), size)

    pl.semaphore_wait(barrier, count_e + count_z - 2)

    def scatter(d):
        to = (e + d) % count_e
        return pltpu.make_async_remote_copy(
            src_ref=packed.at[rows_of(to), :], dst_ref=parts.at[d], send_sem=s1.at[d], recv_sem=r1.at[d],
            device_id=(g, to, z), device_id_type=MESH)

    def share(d):
        to = (z + d) % count_z
        return pltpu.make_async_remote_copy(
            src_ref=sums.at[0], dst_ref=sums.at[d], send_sem=s2.at[d], recv_sem=r2.at[d],
            device_id=(g, e, to), device_id_type=MESH)

    def gather(d):
        to = (e + d) % count_e
        return pltpu.make_async_remote_copy(
            src_ref=gram_ref.at[rows_of(e), :], dst_ref=gram_ref.at[rows_of(e), :], send_sem=s3.at[d], recv_sem=r3.at[d],
            device_id=(g, to, z), device_id_type=MESH)

    for d in range(1, count_e):
        scatter(d).start()
    total = packed[rows_of(e), :]
    for d in range(1, count_e):
        scatter(d).wait_recv()
        total = total + parts[d]
    sums[0] = total
    for d in range(1, count_z):
        share(d).start()
    for d in range(1, count_z):
        share(d).wait_recv()
    total = None
    for i in range(count_z):
        part = sums[(z + count_z - i) % count_z]
        total = part if total is None else total + part
    gram_ref[rows_of(e), :] = total
    for d in range(1, count_e):
        gather(d).start()
    for d in range(1, count_e):
        gather(d).wait_recv()
    for d in range(1, count_e):
        scatter(d).wait_send()
        gather(d).wait_send()
    for d in range(1, count_z):
        share(d).wait_send()


def make_series(lat_index, metric_table, coherent, buf, col, count_e, count_z):
    fields, padded_rows, epochs, wc = buf.shape
    smem, vmem = pl.BlockSpec(memory_space=pltpu.SMEM), pl.BlockSpec(memory_space=pltpu.VMEM)
    dma = pltpu.SemaphoreType.DMA
    lines = len(packed_blocks(epochs)) * LANES
    return pl.pallas_call(
        functools.partial(series_kernel, count_e, count_z),
        out_shape=(
            jax.ShapeDtypeStruct((3, padded_rows - 2, epochs, wc), jnp.float32),
            jax.ShapeDtypeStruct((lines, LANES), jnp.float32),
        ),
        in_specs=[smem, smem, vmem, vmem, vmem],
        out_specs=(vmem, vmem),
        scratch_shapes=[
            pltpu.VMEM((lines, LANES), jnp.float32),
            pltpu.VMEM((count_e, lines // count_e, LANES), jnp.float32),
            pltpu.VMEM((count_z, lines // count_e, LANES), jnp.float32),
            dma((count_e,)), dma((count_e,)), dma((count_z,)), dma((count_z,)),
            dma((count_e,)), dma((count_e,)),
        ],
        compiler_params=pltpu.CompilerParams(
            collective_id=1, has_side_effects=True, vmem_limit_bytes=VMEM_LIMIT),
        name="series",
    )(lat_index, metric_table, coherent, buf, col)


def leaf_inverse(block):
    n = block.shape[0]
    i = lax.broadcasted_iota(jnp.int32, (n, LANES), 0)
    j = lax.broadcasted_iota(jnp.int32, (n, LANES), 1)
    eye = (j == i + n).astype(jnp.float32)
    pad = jnp.zeros((n, LANES - n), jnp.float32)
    work = jnp.concatenate([block, pad], axis=1) + eye
    pivots = jnp.ones((n, LANES), jnp.float32)
    for start in range(0, n, SUB):
        held = [jnp.broadcast_to(work[:, c:c + 1], (n, LANES)) for c in range(start, start + SUB)]
        for c in range(start, start + SUB):
            column = held[c - start]
            pivot = column[c:c + 1, :]
            factor = jnp.where(i > c, column * (1.0 / pivot), 0.0)
            pivots = jnp.where(i == c, pivot, pivots)
            for k in range(c + 1, start + SUB):
                held[k - start] = held[k - start] - factor * held[k - start][c:c + 1, :]
            work = work - factor * work[c:c + 1, :]
    return (work * lax.rsqrt(pivots))[:, n:2 * n]


def packed_blocks(epochs):
    n = epochs // LANES
    return [(i, j) for i in range(n) for j in range(i, n)]


def scores_kernel(count, s_ref, gram_ref, r_ref, out_ref, work, held, done, fetch, flush):
    epochs = r_ref.shape[0]
    rows, wc = s_ref.shape[1], s_ref.shape[3]
    fetches = [pltpu.make_async_copy(s_ref.at[k], held.at[k], fetch.at[k]) for k in range(3)]
    for copy in fetches:
        copy.start()
    i = lax.broadcasted_iota(jnp.int32, (epochs, epochs), 0)
    j = lax.broadcasted_iota(jnp.int32, (epochs, epochs), 1)
    eye = (i == j).astype(jnp.float32)
    work[:, :epochs] = 0.05 * eye
    work[:, epochs:] = eye
    for at, (bi, bj) in enumerate(packed_blocks(epochs)):
        tile = (pl.ds(bi * LANES, LANES), pl.ds(bj * LANES, LANES))
        work[tile] = work[tile] + gram_ref[at * LANES:(at + 1) * LANES, :] * (1.0 / count)
    for start in range(0, epochs, LEAF):
        stop = start + LEAF
        first = start // LANES * LANES
        last = min(first + LANES, epochs) + epochs
        inner = leaf_inverse(work[start:stop, start:stop])
        now = jnp.dot(inner, work[start:stop, first:last], precision=HIGHEST, preferred_element_type=jnp.float32)
        work[start:stop, first:last] = now
        if stop < epochs:
            base = stop // LANES * LANES
            head = now[:, base - first:epochs - first]
            update = lax.dot_general(
                head, now, (((0,), (0,)), ((), ())), precision=HIGHEST, preferred_element_type=jnp.float32)
            work[stop:, first:last] = work[stop:, first:last] - update[stop - base:, :]
    r_ref[...] = jnp.where(i <= j, work[:, :epochs], 0.0)
    whiten = jnp.where(i >= j, work[:, epochs:], 0.0)
    tiles = wc // LANES
    flushes = []
    for k in range(3):
        fetches[k].wait()
        for r in range(rows):
            result = jnp.dot(whiten, held[k, r], precision=HIGHEST, preferred_element_type=jnp.float32)
            for c in range(tiles):
                done[k, pl.ds(c * rows + r, epochs, stride=tiles * rows), :] = result[:, c * LANES:(c + 1) * LANES]
        flushes.append(pltpu.make_async_copy(done.at[k], out_ref.at[k], flush.at[k]))
        flushes[-1].start()
    for copy in flushes:
        copy.wait()


def make_scores(series, gram, count):
    _, rows, epochs, wc = series.shape
    lines = epochs * rows * wc // LANES
    vmem, anywhere = pl.BlockSpec(memory_space=pltpu.VMEM), pl.BlockSpec(memory_space=pl.ANY)
    rfactor, scores = pl.pallas_call(
        functools.partial(scores_kernel, count),
        out_shape=(
            jax.ShapeDtypeStruct((epochs, epochs), jnp.float32),
            jax.ShapeDtypeStruct((3, lines, LANES), jnp.float32),
        ),
        in_specs=[anywhere, vmem],
        out_specs=(vmem, anywhere),
        scratch_shapes=[
            pltpu.VMEM((epochs, 2 * epochs), jnp.float32),
            pltpu.VMEM(series.shape, jnp.float32),
            pltpu.VMEM((3, lines, LANES), jnp.float32),
            pltpu.SemaphoreType.DMA((3,)),
            pltpu.SemaphoreType.DMA((3,)),
        ],
        compiler_params=pltpu.CompilerParams(vmem_limit_bytes=VMEM_LIMIT),
        name="scores",
    )(series, gram)
    scores = scores.reshape(3, epochs, wc // LANES, rows, LANES)
    return rfactor, scores.transpose(0, 1, 3, 2, 4).reshape(3, epochs, rows, wc)


def on_device(count_e, count_z, east_velocity, up_velocity, metric_table, lat_index, coherent):
    velocity = jnp.stack([east_velocity, up_velocity]).transpose(0, 2, 1, 3)
    fields, rows, te, columns = velocity.shape
    wc = columns // count_e
    blank = jnp.zeros((fields, rows, te, 1), jnp.float32)
    left = jnp.concatenate([blank, velocity[..., wc - 1:columns - 1:wc]], axis=3)
    right = jnp.concatenate([velocity[..., wc:columns:wc], blank], axis=3)
    edge = jnp.stack([left, right], axis=2).reshape(2 * fields * rows, te, count_e).transpose(2, 1, 0)
    edge = jnp.pad(edge, ((0, 0), (0, 0), (0, LANES - 2 * fields * rows)))
    buf, col = exchange(velocity, edge, count_e, count_z)
    series, gram = make_series(lat_index, metric_table, coherent, buf, col, count_e, count_z)
    return make_scores(series, gram, 3 * rows * count_z * columns)


def solution(mesh):
    in_specs = (
        P("epoch", ("groups", "tile"), None),
        P("epoch", ("groups", "tile"), None),
        P(),
        P(("groups", "tile")),
        P(("groups", "tile"), "epoch"),
    )
    out_specs = (P("groups", None), P(None, None, ("groups", "tile"), "epoch"))
    return jax.shard_map(
        functools.partial(on_device, mesh.shape["epoch"], mesh.shape["tile"]),
        mesh=mesh, in_specs=in_specs, out_specs=out_specs, check_vma=False,
    )
```

time: 88.7 us -> 77.9 us (0.88)
  Pallas kernels: 80.3 us -> 71.1 us
  local copies, waits for them, and re-layouts: 7.11 us -> 5.47 us
    pallas_call x2 -> x1, Pallas kernels: 26.7 us -> 21.1 us  [make_series(): pl.pallas_call(functools.partial(series_kernel, count_e, count_z), out_sh...]
    pallas_call x1, Pallas kernels: 36.5 us -> 33 us  [exchange(): pl.pallas_call(functools.partial(exchange_kernel, count_e, count_z), out_...]
    unnamed x14 -> x10, local copies, waits for them, and re-layouts: 2.56 us -> 0.92 us
where the time goes in v1:
time: 77.9 us; the launch traced here: 77.7 us
  Pallas kernels  71.1 us (91%)
  local copies, waits for them, and re-layouts  5.47 us (7%)
  between operations  0.93 us (1%)
    pallas_call x1, Pallas kernels, exchange(): pl.pallas_call(functools.partial(exchange_kernel, count_e, count_z), out_...  33 us
    pallas_call x1, Pallas kernels, make_series(): pl.pallas_call(functools.partial(series_kernel, count_e, count_z), out_sh...  21.1 us
    pallas_call x1, Pallas kernels, make_scores(): pl.pallas_call(functools.partial(scores_kernel, count), out_shape=(jax.Sh...  17 us
    another operation x1, local copies, waits for them, and re-layouts, on_device(): velocity = jnp.stack([east_velocity, up_velocity]).transpose(0, 2, 1, 3)  2.76 us

profile of v1, /device:TPU:0, one launch (start us, length us, event | category | flops | bytes accessed | tf_op | source)
XLA Modules:
  0.0 77.7 jit_solution(10629910497966339255)
XLA Ops:
  0.6 2.8 %copy_bitcast_fusion = (f32[1,64,2,2048]{3,1,2,0:T(8,128)S(1)}, f32[1,64,2,2048]{3,1,2,0:T(8,128)S(1)}) fusion(f32[64,2,2048]{2,1,0:T(2,128)} %param.6, f32[64,2,2048]{2,1,0:T(2,128)} %param.5), kind=kLoop, calls=%fused_computation.1 | loop fusion | bytes 4194304 | tf_op jit(solution)/shard_map/stack | solution.py:409
  3.4 0.2 maximum_bitcast_fusion.v_ref
  3.6 0.0 copy-start.4
  3.6 0.4 slice.7
  4.0 0.0 copy-start.1
  4.0 0.0 copy-start.2
  4.0 0.0 copy-start.3
  4.1 0.4 slice.6
  4.5 0.1 pad_bitcast_fusion.1
  4.6 0.1 copy.25
  4.7 0.1 copy.26
  4.9 0.7 pad.6.edge_ref
  5.5 0.0 copy-done.4
  5.5 33.0 %exchange.1 = (f32[2,4,256,512]{3,2,1,0:T(8,128)}, f32[256,128]{1,0:T(8,128)}) custom-call(f32[2,2,64,2048]{3,2,1,0:T(8,128)} %copy-done.4, f32[4,64,128]{2,1,0:T(8,128)} %pad.6.edge_ref), custom_call_target="tpu_custom_call" | custom-call | tf_op jit(solution)/shard_map/exchange/pallas_call | solution.py:159
  38.5 0.0 copy-done.1
  38.6 0.0 copy-done.2
  38.6 0.0 copy-done.3
  38.6 0.0 copy-start
  38.6 0.9 %copy-done = f32[256,128]{1,0:T(8,128)S(1)} copy-done((f32[256,128]{1,0:T(8,128)S(1)}, f32[256,128]{1,0:T(8,128)}, u32[]{:S(2)}) %copy-start) | copy-done | bytes 131096
  39.5 21.1 %series.1 = (f32[3,2,256,512]{3,2,1,0:T(8,128)S(1)}, f32[384,128]{1,0:T(8,128)S(1)}) custom-call(s32[2]{0:T(128)S(1)} %copy-done.2, f32[64]{0:T(128)S(1)} %copy-done.3, s32[2,512]{1,0:T(2,128)S(1)} %copy-done.1, f32[2,4,256,512]{3,2,1,0:T(8,128)} %get-tuple-element.8.buf_ref, f32[256,128]{1,0:T(8,128)S(1)} %copy-done), custom_call_target="tpu_custom_call" | custom-call | tf_op jit(solution)/shard_map/series/pallas_call | solution.py:292
  60.6 17.0 %scores.1 = (f32[256,256]{1,0:T(8,128)}, f32[3,2048,128]{2,1,0:T(8,128)}) custom-call(f32[3,2,256,512]{3,2,1,0:T(8,128)S(1)} %get-tuple-element.10.s_ref, f32[384,128]{1,0:T(8,128)S(1)} %get-tuple-element.11.gram_ref), custom_call_target="tpu_custom_call" | custom-call | tf_op jit(solution)/shard_map/scores/pallas_call | solution.py:386
  (2 shorter events, 0.0 us)
Async XLA Ops:
  3.6 1.9 %copy-start.4 = (f32[2,2,64,2048]{3,2,1,0:T(8,128)}, f32[2,2,64,2048]{3,2,1,0:T(8,128)S(1)}, u32[]{:S(2)}) copy-start(f32[2,2,64,2048]{3,2,1,0:T(8,128)S(1)} %maximum_bitcast_fusion.v_ref) | copy-start | bytes 6291460
  4.0 34.5 %copy-start.1 = (s32[2,512]{1,0:T(2,128)S(1)}, s32[2,512]{1,0:T(2,128)}, u32[]{:S(2)}) copy-start(s32[2,512]{1,0:T(2,128)} %coh_ref.1) | copy-start | bytes 12292
  4.0 34.5 %copy-start.2 = (s32[2]{0:T(128)S(1)}, s32[2]{0:T(128)}, u32[]{:S(2)}) copy-start(s32[2]{0:T(128)} %lat_ref.1) | copy-start | bytes 28
  4.0 34.5 %copy-start.3 = (f32[64]{0:T(128)S(1)}, f32[64]{0:T(128)}, u32[]{:S(2)}) copy-start(f32[64]{0:T(128)} %table_ref.1) | copy-start | bytes 772
  38.6 0.9 %copy-start = (f32[256,128]{1,0:T(8,128)S(1)}, f32[256,128]{1,0:T(8,128)}, u32[]{:S(2)}) copy-start(f32[256,128]{1,0:T(8,128)} %get-tuple-element.9.col_ref) | copy-start | bytes 393220

commit v2 on v1

--- a/solution.py
+++ b/solution.py
@@ -10,10 +10,10 @@
 MESH = pl.DeviceIdType.MESH
 HIGHEST = lax.Precision.HIGHEST
 LANES = 128
-LEAF = 32
-SUB = 8
+LEAF = 64
+SUB = 16
 PIECES = 2
-WINDOW = 2
+WINDOW = 8
 VMEM_LIMIT = 48 * 1024 * 1024
 
 
@@ -75,7 +75,7 @@
     def edges(d):
         to = target(d)
         return pltpu.make_async_remote_copy(
-            src_ref=edge_ref.at[to], dst_ref=col_ref.at[times(e), :],
+            src_ref=edge_ref.at[to], dst_ref=col_ref.at[e],
             send_sem=edge_send.at[d], recv_sem=edge_recv.at[d],
             device_id=(g, to, z), device_id_type=MESH,
         )
@@ -117,7 +117,7 @@
         for r in range(rows):
             own.append(pltpu.make_async_copy(
                 v_ref.at[f, r, :, cols(e)], buf_ref.at[f, r + 1, times(e), :], local.at[f * rows + r]))
-    own.append(pltpu.make_async_copy(edge_ref.at[e], col_ref.at[times(e), :], local.at[fields * rows]))
+    own.append(pltpu.make_async_copy(edge_ref.at[e], col_ref.at[e], local.at[fields * rows]))
     for copy in own:
         copy.start()
     for c in range(len(chunks)):
@@ -160,15 +160,16 @@
         functools.partial(exchange_kernel, count_e, count_z),
         out_shape=(
             jax.ShapeDtypeStruct((fields, rows + 2, te * count_e, wc), jnp.float32),
-            jax.ShapeDtypeStruct((te * count_e, LANES), jnp.float32),
+            jax.ShapeDtypeStruct(edge.shape, jnp.float32),
         ),
         in_specs=[pl.BlockSpec(memory_space=pl.ANY)] * 2,
-        out_specs=(pl.BlockSpec(memory_space=pl.ANY),) * 2,
+        out_specs=(pl.BlockSpec(memory_space=pltpu.VMEM),) * 2,
         scratch_shapes=[
             dma((count_e, n * PIECES)), dma((count_e, n * PIECES)), dma((count_e,)), dma((count_e,)),
             dma((2, count_e, fields * PIECES)), dma((2, count_e, fields * PIECES)), dma((n + 1,)),
         ],
-        compiler_params=pltpu.CompilerParams(collective_id=0, has_side_effects=True),
+        compiler_params=pltpu.CompilerParams(
+            collective_id=0, has_side_effects=True, vmem_limit_bytes=VMEM_LIMIT // 4),
         name="exchange",
     )(velocity, edge)
 
@@ -194,11 +195,14 @@
     steps = lax.broadcasted_iota(jnp.int32, (epochs, 1), 0).astype(jnp.float32) - (epochs - 1) / 2.0
     squares = epochs * (epochs * epochs - 1) / 12.0
 
+    te = epochs // count_e
+    col = jnp.concatenate([col_ref[source].T[:te, :] for source in range(count_e)], axis=0)
+
     def along_x(f, r):
         x = buf_ref[f, r + 1]
         at = (f * rows + r) * 2
-        right = jnp.where(lane == wc - 1, col_ref[:, at + 1:at + 2], pltpu.roll(x, wc - 1, 1))
-        left = jnp.where(lane == 0, col_ref[:, at:at + 1], pltpu.roll(x, 1, 1))
+        right = jnp.where(lane == wc - 1, col[:, at + 1:at + 2], pltpu.roll(x, wc - 1, 1))
+        left = jnp.where(lane == 0, col[:, at:at + 1], pltpu.roll(x, 1, 1))
         return 0.5 * (right - left)
 
     def row(f, i):
@@ -305,7 +309,7 @@
             dma((count_e,)), dma((count_e,)),
         ],
         compiler_params=pltpu.CompilerParams(
-            collective_id=1, has_side_effects=True, vmem_limit_bytes=VMEM_LIMIT),
+            collective_id=1, has_side_effects=True, vmem_limit_bytes=VMEM_LIMIT // 2),
         name="series",
     )(lat_index, metric_table, coherent, buf, col)
 
@@ -412,8 +416,8 @@
     blank = jnp.zeros((fields, rows, te, 1), jnp.float32)
     left = jnp.concatenate([blank, velocity[..., wc - 1:columns - 1:wc]], axis=3)
     right = jnp.concatenate([velocity[..., wc:columns:wc], blank], axis=3)
-    edge = jnp.stack([left, right], axis=2).reshape(2 * fields * rows, te, count_e).transpose(2, 1, 0)
-    edge = jnp.pad(edge, ((0, 0), (0, 0), (0, LANES - 2 * fields * rows)))
+    edge = jnp.stack([left, right], axis=2).reshape(2 * fields * rows, te, count_e).transpose(2, 0, 1)
+    edge = jnp.pad(edge, ((0, 0), (0, 0), (0, -te % LANES)))
     buf, col = exchange(velocity, edge, count_e, count_z)
     series, gram = make_series(lat_index, metric_table, coherent, buf, col, count_e, count_z)
     return make_scores(series, gram, 3 * rows * count_z * columns)

time: 77.9 us -> 70.2 us (0.901)
  Pallas kernels: 71.1 us -> 65.1 us
  local copies, waits for them, and re-layouts: 5.47 us -> 3.8 us
    pallas_call x1, Pallas kernels: 17 us -> 13.8 us  [make_scores(): pl.pallas_call(functools.partial(scores_kernel, count), out_shape=(jax.Sh...]
    pallas_call x1, Pallas kernels: 33 us -> 31.3 us  [exchange(): pl.pallas_call(functools.partial(exchange_kernel, count_e, count_z), out_...]
    pallas_call x1, Pallas kernels: 21.1 us -> 20 us  [make_series(): pl.pallas_call(functools.partial(series_kernel, count_e, count_z), out_sh...]
    unnamed x10 -> x6, local copies, waits for them, and re-layouts: 0.92 us -> 0.02 us
where the time goes in v2:
time: 70.2 us; the launch traced here: 70.1 us
  Pallas kernels  65.1 us (93%)
  local copies, waits for them, and re-layouts  3.8 us (5%)
  between operations  0.9 us (1%)
    pallas_call x1, Pallas kernels, exchange(): pl.pallas_call(functools.partial(exchange_kernel, count_e, count_z), out_...  31.3 us
    pallas_call x1, Pallas kernels, make_series(): pl.pallas_call(functools.partial(series_kernel, count_e, count_z), out_sh...  20 us
    pallas_call x1, Pallas kernels, make_scores(): pl.pallas_call(functools.partial(scores_kernel, count), out_shape=(jax.Sh...  13.8 us
    another operation x1, local copies, waits for them, and re-layouts, on_device(): velocity = jnp.stack([east_velocity, up_velocity]).transpose(0, 2, 1, 3)  2.76 us

profile of v2, /device:TPU:0, one launch (start us, length us, event | category | flops | bytes accessed | tf_op | source)
XLA Modules:
  0.0 70.1 jit_solution(7761887757764612067)
XLA Ops:
  0.6 2.8 %copy_bitcast_fusion = (f32[1,64,2,2048]{3,1,2,0:T(8,128)S(1)}, f32[1,64,2,2048]{3,1,2,0:T(8,128)S(1)}) fusion(f32[64,2,2048]{2,1,0:T(2,128)} %param.6, f32[64,2,2048]{2,1,0:T(2,128)} %param.5), kind=kLoop, calls=%fused_computation.1 | loop fusion | bytes 4194304 | tf_op jit(solution)/shard_map/stack | solution.py:413
  3.4 0.2 maximum_bitcast_fusion.v_ref
  3.6 0.0 copy-start
  3.6 0.0 copy-start.1
  3.6 0.0 copy-start.2
  3.7 0.4 slice.7
  4.1 0.4 slice.6
  4.5 0.1 pad_bitcast_fusion.1
  4.6 0.1 copy.19
  4.7 31.3 %exchange.1 = (f32[2,4,256,512]{3,2,1,0:T(8,128)S(1)}, f32[4,8,128]{2,1,0:T(8,128)S(1)}) custom-call(f32[2,2,64,2048]{3,2,1,0:T(8,128)S(1)} %maximum_bitcast_fusion.v_ref, f32[4,8,128]{2,1,0:T(8,128)S(1)} %pad.6.edge_ref), custom_call_target="tpu_custom_call" | custom-call | tf_op jit(solution)/shard_map/exchange/pallas_call | solution.py:159
  36.0 0.0 copy-done
  36.1 0.0 copy-done.1
  36.1 0.0 copy-done.2
  36.1 20.0 %series.1 = (f32[3,2,256,512]{3,2,1,0:T(8,128)S(1)}, f32[384,128]{1,0:T(8,128)S(1)}) custom-call(s32[2]{0:T(128)S(1)} %copy-done.1, f32[64]{0:T(128)S(1)} %copy-done.2, s32[2,512]{1,0:T(2,128)S(1)} %copy-done, f32[2,4,256,512]{3,2,1,0:T(8,128)S(1)} %get-tuple-element.8.buf_ref, f32[4,8,128]{2,1,0:T(8,128)S(1)} %get-tuple-element.9.col_ref), custom_call_target="tpu_custom_call" | custom-call | tf_op jit(solution)/shard_map/series/pallas_call | solution.py:296
  56.1 13.8 %scores.1 = (f32[256,256]{1,0:T(8,128)}, f32[3,2048,128]{2,1,0:T(8,128)}) custom-call(f32[3,2,256,512]{3,2,1,0:T(8,128)S(1)} %get-tuple-element.10.s_ref, f32[384,128]{1,0:T(8,128)S(1)} %get-tuple-element.11.gram_ref), custom_call_target="tpu_custom_call" | custom-call | tf_op jit(solution)/shard_map/scores/pallas_call | solution.py:390
  (3 shorter events, 0.0 us)
Async XLA Ops:
  3.6 32.4 %copy-start = (s32[2,512]{1,0:T(2,128)S(1)}, s32[2,512]{1,0:T(2,128)}, u32[]{:S(2)}) copy-start(s32[2,512]{1,0:T(2,128)} %coh_ref.1) | copy-start | bytes 12292
  3.6 32.4 %copy-start.1 = (s32[2]{0:T(128)S(1)}, s32[2]{0:T(128)}, u32[]{:S(2)}) copy-start(s32[2]{0:T(128)} %lat_ref.1) | copy-start | bytes 28
  3.6 32.4 %copy-start.2 = (f32[64]{0:T(128)S(1)}, f32[64]{0:T(128)}, u32[]{:S(2)}) copy-start(f32[64]{0:T(128)} %table_ref.1) | copy-start | bytes 772
